TPU v7x, 32 devices: a whole 2x2x4 slice. The times are simulated.
32 devices in a mesh: groups: 2 (over x), seq: 16 (over z, y, core).
Axes of the slice: x: 2, y: 2, z: 4, core: 2. Of those that a mesh axis runs over, the one named last changes fastest.
Arguments:
- queries: bfloat16 [8192, 2048], P(('groups', 'seq')), parts along dimension 0, may hold values from -6 to 6
- keys: bfloat16 [8192, 2048], P(('groups', 'seq')), parts along dimension 0, may hold values from -6 to 6
- values: bfloat16 [8192, 2048], P(('groups', 'seq')), parts along dimension 0, may hold values from -6 to 6
- gain: float32 [2048], replicated, may hold values from 0.1 to 1.9
Outputs:
- attended: bfloat16 [8192, 2048], P(('groups', 'seq')), parts along dimension 0
There are 2 independent parts, one for each index of `groups`. A program takes and returns all parts, laid end to end along the dimension named above; an argument that names none is the same for every part. Nothing has to cross between parts.
All inputs are finite; a program needn't handle non-finite values.
Results may differ from a plain program's by a relative error of at most 0.01.
Values may be sent and summed in bfloat16 or wider, within the bound.
A program may use at most 192 MiB of HBM per device.

v0:
```python
import jax
import jax.numpy as jnp
from jax import lax
from jax.sharding import PartitionSpec as P

HEADS = 32
HEAD_DIM = 64


def entering(shard, axis, combine, identity):
    size, here = (lax.axis_size(axis), lax.axis_index(axis))
    everything = lax.all_gather(shard.astype(jnp.bfloat16), axis)
    start = jnp.broadcast_to(jnp.asarray(identity, shard.dtype), shard.shape)

    def hop(k, before):
        reached = k < here
        new = combine(before, everything[k].astype(shard.dtype))
        return jnp.where(reached, new, before)

    return lax.fori_loop(0, size, hop, start)


def add_states(earlier, later):
    return earlier + later


def on_device(queries, keys, values, gain):
    count = queries.shape[0]
    fq = jax.nn.relu(queries).reshape(count, HEADS, HEAD_DIM)
    fk = jax.nn.relu(keys).reshape(count, HEADS, HEAD_DIM)
    vals = values.reshape(count, HEADS, HEAD_DIM)
    state = jnp.einsum("thd,the->hde", fk, vals, preferred_element_type=jnp.float32)
    zero_state = jnp.zeros_like(state)
    prior = entering(state, "seq", add_states, zero_state)
    prior_b = prior.astype(jnp.bfloat16)
    inter = jnp.einsum("thd,hde->the", fq, prior_b, preferred_element_type=jnp.float32)
    rows = jnp.arange(count)[:, None]
    cols = jnp.arange(count)[None, :]
    causal = cols <= rows
    width = HEADS // 4
    pieces = []
    for group in range(4):
        q_grp = fq[:, group * width : (group + 1) * width]
        k_grp = fk[:, group * width : (group + 1) * width]
        v_grp = vals[:, group * width : (group + 1) * width]
        scores = jnp.einsum("thd,shd->hts", q_grp, k_grp, preferred_element_type=jnp.float32)
        scores = jnp.where(causal[None], scores, 0.0).astype(jnp.bfloat16)
        pieces.append(jnp.einsum("hts,she->the", scores, v_grp, preferred_element_type=jnp.float32))
    intra = jnp.concatenate(pieces, axis=1)
    numer = inter + intra
    mean_sq = jnp.mean(numer * numer, axis=-1, keepdims=True)
    normed = numer * lax.rsqrt(mean_sq + 1e-05)
    normed = normed.reshape(count, HEADS * HEAD_DIM) * gain[None, :]
    return normed.astype(jnp.bfloat16)


def solution(mesh):
    return jax.shard_map(
        on_device,
        mesh=mesh,
        in_specs=(
            P(("groups", "seq"), None),
            P(("groups", "seq"), None),
            P(("groups", "seq"), None),
            P(),
        ),
        out_specs=P(("groups", "seq"), None),
        check_vma=False,
    )
```

profile of v0, /device:TPU:0, one launch (start us, length us, event | category | flops | bytes accessed | tf_op | source)
XLA Modules:
  0.0 128.4 jit_solution(8930667809056329429)
XLA Ops:
  6.5 0.0 all-gather.3.cloned.1.call-start
  6.5 1.5 %copy.15 = bf16[256,2048]{0,1:T(8,128)(2,1)S(1)} copy(bf16[256,2048]{1,0:T(8,128)(2,1)} %param.7) | data formatting | bytes 2097152 | tf_op args[1]
  8.0 0.1 broadcast_maximum_fusion.1
  8.1 1.5 %copy.16 = bf16[256,2048]{0,1:T(8,128)(2,1)S(1)} copy(bf16[256,2048]{1,0:T(8,128)(2,1)} %param.8) | data formatting | bytes 2097152 | tf_op args[2]
  9.6 1.3 convolution_convert_fusion
  10.8 0.0 all-gather.3.cloned.1.call-update
  10.9 2.3 %copy.17 = bf16[256,2048]{0,1:T(8,128)(2,1)} copy(bf16[256,2048]{1,0:T(8,128)(2,1)} %param.6) | data formatting | bytes 2097152 | tf_op args[0]
  13.2 1.3 %broadcast_maximum_fusion = bf16[256,2048]{0,1:T(8,128)(2,1)S(1)} fusion(bf16[256,2048]{0,1:T(8,128)(2,1)} %copy.17), kind=kLoop, calls=%fused_computation.15 | loop fusion | flops 524288 | bytes 2097152 | tf_op jit(solution)/shard_map/jit(relu)/max | solution.py:29
  14.5 0.0 copy-start
  14.5 0.5 select_convert_fusion
  15.0 1.3 convolution_bitcast_fusion
  16.3 0.5 select_convert_fusion.1
  16.7 1.3 convolution_bitcast_fusion.1
  18.0 0.5 select_convert_fusion.2
  18.5 1.2 convolution_bitcast_fusion.2
  19.8 0.0 copy-done
  19.8 0.5 select_convert_fusion.3
  20.2 1.2 convolution_bitcast_fusion.3
  21.5 67.2 %all-gather.3.cloned.1.call-done = bf16[512,64,64]{2,1,0:T(8,128)(2,1)} async-done(((bf16[32,64,64]{2,1,0:T(8,128)(2,1)}), bf16[512,64,64]{2,1,0:T(8,128)(2,1)}) %all-gather.3.cloned.1.call-update) | async-done | bytes 4194320 | tf_op jit(solution)/shard_map/all_gather | solution.py:12
  88.6 0.0 copy-start.1
  88.6 0.0 copy-start.2
  88.6 0.0 copy-start.3
  88.6 26.2 %while.14 = (s32[]{:T(128)}, f32[32,64,64]{2,1,0:T(8,128)S(1)}, s32[]{:T(128)}, bf16[16,32,64,64]{3,2,1,0:T(8,128)(2,1)}, s32[]{:T(128)}, /*index=5*/s32[]{:T(128)}) while((s32[]{:T(128)}, f32[32,64,64]{2,1,0:T(8,128)S(1)}, s32[]{:T(128)}, bf16[16,32,64,64]{3,2,1,0:T(8,128)(2,1)}, s32[]{:T(128)}, /*index=5*/s32[]{:T(128)}) %tuple.38), condition=%wide.region_1.2_spmd.clone, body=%wide.region_0.1_spmd.clone.sunk | while | flops 524292 | bytes 1310813 | solution.py:20
  88.6 1.8 %add_select_fusion.2 = f32[32,64,64]{2,1,0:T(8,128)S(1)} fusion(f32[32,64,64]{2,1,0:T(8,128)S(1)} %get-tuple-element.142, bf16[16,32,64,64]{3,2,1,0:T(8,128)(2,1)} %get-tuple-element.150, s32[]{:T(128)} %get-tuple-element.141, pred[]{:T(512)S(6)} %compare.3, pred[]{:T(512)S(6)} %lt.21), kind=kLoop, calls=%fused_computation.clone.1 | loop fusion | flops 524288 | bytes 1310726 | tf_op jit(solution)/shard_map/while/body/eval_jaxpr/jit(_where)/select_n | solution.py:18
  90.4 1.6 %add_select_fusion.2 = f32[32,64,64]{2,1,0:T(8,128)S(1)} fusion(f32[32,64,64]{2,1,0:T(8,128)S(1)} %get-tuple-element.142, bf16[16,32,64,64]{3,2,1,0:T(8,128)(2,1)} %get-tuple-element.150, s32[]{:T(128)} %get-tuple-element.141, pred[]{:T(512)S(6)} %compare.3, pred[]{:T(512)S(6)} %lt.21), kind=kLoop, calls=%fused_computation.clone.1 | loop fusion | flops 524288 | bytes 1310726 | tf_op jit(solution)/shard_map/while/body/eval_jaxpr/jit(_where)/select_n | solution.py:18
  92.0 1.6 %add_select_fusion.2 = f32[32,64,64]{2,1,0:T(8,128)S(1)} fusion(f32[32,64,64]{2,1,0:T(8,128)S(1)} %get-tuple-element.142, bf16[16,32,64,64]{3,2,1,0:T(8,128)(2,1)} %get-tuple-element.150, s32[]{:T(128)} %get-tuple-element.141, pred[]{:T(512)S(6)} %compare.3, pred[]{:T(512)S(6)} %lt.21), kind=kLoop, calls=%fused_computation.clone.1 | loop fusion | flops 524288 | bytes 1310726 | tf_op jit(solution)/shard_map/while/body/eval_jaxpr/jit(_where)/select_n | solution.py:18
  93.7 1.6 %add_select_fusion.2 = f32[32,64,64]{2,1,0:T(8,128)S(1)} fusion(f32[32,64,64]{2,1,0:T(8,128)S(1)} %get-tuple-element.142, bf16[16,32,64,64]{3,2,1,0:T(8,128)(2,1)} %get-tuple-element.150, s32[]{:T(128)} %get-tuple-element.141, pred[]{:T(512)S(6)} %compare.3, pred[]{:T(512)S(6)} %lt.21), kind=kLoop, calls=%fused_computation.clone.1 | loop fusion | flops 524288 | bytes 1310726 | tf_op jit(solution)/shard_map/while/body/eval_jaxpr/jit(_where)/select_n | solution.py:18
  95.3 1.6 %add_select_fusion.2 = f32[32,64,64]{2,1,0:T(8,128)S(1)} fusion(f32[32,64,64]{2,1,0:T(8,128)S(1)} %get-tuple-element.142, bf16[16,32,64,64]{3,2,1,0:T(8,128)(2,1)} %get-tuple-element.150, s32[]{:T(128)} %get-tuple-element.141, pred[]{:T(512)S(6)} %compare.3, pred[]{:T(512)S(6)} %lt.21), kind=kLoop, calls=%fused_computation.clone.1 | loop fusion | flops 524288 | bytes 1310726 | tf_op jit(solution)/shard_map/while/body/eval_jaxpr/jit(_where)/select_n | solution.py:18
  96.9 1.6 %add_select_fusion.2 = f32[32,64,64]{2,1,0:T(8,128)S(1)} fusion(f32[32,64,64]{2,1,0:T(8,128)S(1)} %get-tuple-element.142, bf16[16,32,64,64]{3,2,1,0:T(8,128)(2,1)} %get-tuple-element.150, s32[]{:T(128)} %get-tuple-element.141, pred[]{:T(512)S(6)} %compare.3, pred[]{:T(512)S(6)} %lt.21), kind=kLoop, calls=%fused_computation.clone.1 | loop fusion | flops 524288 | bytes 1310726 | tf_op jit(solution)/shard_map/while/body/eval_jaxpr/jit(_where)/select_n | solution.py:18
  98.6 1.6 %add_select_fusion.2 = f32[32,64,64]{2,1,0:T(8,128)S(1)} fusion(f32[32,64,64]{2,1,0:T(8,128)S(1)} %get-tuple-element.142, bf16[16,32,64,64]{3,2,1,0:T(8,128)(2,1)} %get-tuple-element.150, s32[]{:T(128)} %get-tuple-element.141, pred[]{:T(512)S(6)} %compare.3, pred[]{:T(512)S(6)} %lt.21), kind=kLoop, calls=%fused_computation.clone.1 | loop fusion | flops 524288 | bytes 1310726 | tf_op jit(solution)/shard_map/while/body/eval_jaxpr/jit(_where)/select_n | solution.py:18
  100.2 1.6 %add_select_fusion.2 = f32[32,64,64]{2,1,0:T(8,128)S(1)} fusion(f32[32,64,64]{2,1,0:T(8,128)S(1)} %get-tuple-element.142, bf16[16,32,64,64]{3,2,1,0:T(8,128)(2,1)} %get-tuple-element.150, s32[]{:T(128)} %get-tuple-element.141, pred[]{:T(512)S(6)} %compare.3, pred[]{:T(512)S(6)} %lt.21), kind=kLoop, calls=%fused_computation.clone.1 | loop fusion | flops 524288 | bytes 1310726 | tf_op jit(solution)/shard_map/while/body/eval_jaxpr/jit(_where)/select_n | solution.py:18
  101.8 1.6 %add_select_fusion.2 = f32[32,64,64]{2,1,0:T(8,128)S(1)} fusion(f32[32,64,64]{2,1,0:T(8,128)S(1)} %get-tuple-element.142, bf16[16,32,64,64]{3,2,1,0:T(8,128)(2,1)} %get-tuple-element.150, s32[]{:T(128)} %get-tuple-element.141, pred[]{:T(512)S(6)} %compare.3, pred[]{:T(512)S(6)} %lt.21), kind=kLoop, calls=%fused_computation.clone.1 | loop fusion | flops 524288 | bytes 1310726 | tf_op jit(solution)/shard_map/while/body/eval_jaxpr/jit(_where)/select_n | solution.py:18
  103.4 1.6 %add_select_fusion.2 = f32[32,64,64]{2,1,0:T(8,128)S(1)} fusion(f32[32,64,64]{2,1,0:T(8,128)S(1)} %get-tuple-element.142, bf16[16,32,64,64]{3,2,1,0:T(8,128)(2,1)} %get-tuple-element.150, s32[]{:T(128)} %get-tuple-element.141, pred[]{:T(512)S(6)} %compare.3, pred[]{:T(512)S(6)} %lt.21), kind=kLoop, calls=%fused_computation.clone.1 | loop fusion | flops 524288 | bytes 1310726 | tf_op jit(solution)/shard_map/while/body/eval_jaxpr/jit(_where)/select_n | solution.py:18
  105.1 1.6 %add_select_fusion.2 = f32[32,64,64]{2,1,0:T(8,128)S(1)} fusion(f32[32,64,64]{2,1,0:T(8,128)S(1)} %get-tuple-element.142, bf16[16,32,64,64]{3,2,1,0:T(8,128)(2,1)} %get-tuple-element.150, s32[]{:T(128)} %get-tuple-element.141, pred[]{:T(512)S(6)} %compare.3, pred[]{:T(512)S(6)} %lt.21), kind=kLoop, calls=%fused_computation.clone.1 | loop fusion | flops 524288 | bytes 1310726 | tf_op jit(solution)/shard_map/while/body/eval_jaxpr/jit(_where)/select_n | solution.py:18
  106.7 1.6 %add_select_fusion.2 = f32[32,64,64]{2,1,0:T(8,128)S(1)} fusion(f32[32,64,64]{2,1,0:T(8,128)S(1)} %get-tuple-element.142, bf16[16,32,64,64]{3,2,1,0:T(8,128)(2,1)} %get-tuple-element.150, s32[]{:T(128)} %get-tuple-element.141, pred[]{:T(512)S(6)} %compare.3, pred[]{:T(512)S(6)} %lt.21), kind=kLoop, calls=%fused_computation.clone.1 | loop fusion | flops 524288 | bytes 1310726 | tf_op jit(solution)/shard_map/while/body/eval_jaxpr/jit(_where)/select_n | solution.py:18
  108.3 1.6 %add_select_fusion.2 = f32[32,64,64]{2,1,0:T(8,128)S(1)} fusion(f32[32,64,64]{2,1,0:T(8,128)S(1)} %get-tuple-element.142, bf16[16,32,64,64]{3,2,1,0:T(8,128)(2,1)} %get-tuple-element.150, s32[]{:T(128)} %get-tuple-element.141, pred[]{:T(512)S(6)} %compare.3, pred[]{:T(512)S(6)} %lt.21), kind=kLoop, calls=%fused_computation.clone.1 | loop fusion | flops 524288 | bytes 1310726 | tf_op jit(solution)/shard_map/while/body/eval_jaxpr/jit(_where)/select_n | solution.py:18
  110.0 1.6 %add_select_fusion.2 = f32[32,64,64]{2,1,0:T(8,128)S(1)} fusion(f32[32,64,64]{2,1,0:T(8,128)S(1)} %get-tuple-element.142, bf16[16,32,64,64]{3,2,1,0:T(8,128)(2,1)} %get-tuple-element.150, s32[]{:T(128)} %get-tuple-element.141, pred[]{:T(512)S(6)} %compare.3, pred[]{:T(512)S(6)} %lt.21), kind=kLoop, calls=%fused_computation.clone.1 | loop fusion | flops 524288 | bytes 1310726 | tf_op jit(solution)/shard_map/while/body/eval_jaxpr/jit(_where)/select_n | solution.py:18
  111.6 1.6 %add_select_fusion.2 = f32[32,64,64]{2,1,0:T(8,128)S(1)} fusion(f32[32,64,64]{2,1,0:T(8,128)S(1)} %get-tuple-element.142, bf16[16,32,64,64]{3,2,1,0:T(8,128)(2,1)} %get-tuple-element.150, s32[]{:T(128)} %get-tuple-element.141, pred[]{:T(512)S(6)} %compare.3, pred[]{:T(512)S(6)} %lt.21), kind=kLoop, calls=%fused_computation.clone.1 | loop fusion | flops 524288 | bytes 1310726 | tf_op jit(solution)/shard_map/while/body/eval_jaxpr/jit(_where)/select_n | solution.py:18
  113.2 1.6 %add_select_fusion.2 = f32[32,64,64]{2,1,0:T(8,128)S(1)} fusion(f32[32,64,64]{2,1,0:T(8,128)S(1)} %get-tuple-element.142, bf16[16,32,64,64]{3,2,1,0:T(8,128)(2,1)} %get-tuple-element.150, s32[]{:T(128)} %get-tuple-element.141, pred[]{:T(512)S(6)} %compare.3, pred[]{:T(512)S(6)} %lt.21), kind=kLoop, calls=%fused_computation.clone.1 | loop fusion | flops 524288 | bytes 1310726 | tf_op jit(solution)/shard_map/while/body/eval_jaxpr/jit(_where)/select_n | solution.py:18
  114.8 0.0 copy-done.1
  114.9 0.0 copy-done.2
  114.9 0.0 copy-done.3
  114.9 1.7 %multiply_reduce_fusion = (f32[256,32]{0,1:T(8,128)S(1)}, f32[256,32,64]{0,2,1:T(8,128)S(1)}) fusion(f32[256,8,64]{0,2,1:T(8,128)S(1)} %copy-done.2, f32[256,8,64]{0,2,1:T(8,128)S(1)} %copy-done.3, f32[256,8,64]{0,2,1:T(8,128)} %convolution_bitcast_fusion.2, f32[256,8,64]{0,2,1:T(8,128)} %convolution_bitcast_fusion.3, bf16[256,32,64]{0,2,1:T(8,128)(2,1)S(1)} %bitcast.46, ...), kind=kOutput, calls=%fused_computation.3 | convolution fusion | flops 70377472 | bytes 5799936 | tf_op jit(solution)/shard_map/thd,hde->the/dot_general | solution.py:36
  116.6 0.3 broadcast_multiply_fusion
  116.9 0.0 copy-start.4
  116.9 1.9 %copy.19 = f32[256,2048]{1,0:T(8,128)} copy(f32[256,2048]{0,1:T(8,128)S(1)} %bitcast.36) | data formatting | bytes 4194304 | tf_op jit(solution)/shard_map/reshape | solution.py:53
  118.8 0.0 copy-done.4
  118.8 2.8 %multiply_convert_fusion = bf16[256,2048]{1,0:T(8,128)(2,1)} fusion(f32[256,2048]{1,0:T(8,128)} %copy.19, f32[2048]{0:T(1024)S(1)} %copy-done.4), kind=kLoop, calls=%fused_computation.2 | loop fusion | flops 1048576 | bytes 3153920 | tf_op jit(solution)/shard_map/convert_element_type | solution.py:54
  (3 shorter events, 0.0 us)
Async XLA Ops:
  6.5 82.1 %all-gather.3.cloned.1.call-start = ((), (), s32[]{:S(2)}) async-start(), calls=%async_computation | async-start | bytes 8912896 | tf_op jit(solution)/shard_map/all_gather | solution.py:12
  14.5 5.3 %copy-start = (bf16[256,2048]{0,1:T(8,128)(2,1)}, bf16[256,2048]{0,1:T(8,128)(2,1)S(1)}, u32[]{:S(2)}) copy-start(bf16[256,2048]{0,1:T(8,128)(2,1)S(1)} %broadcast_maximum_fusion) | copy-start | bytes 3145732
  88.6 26.2 %copy-start.1 = (bf16[256,2048]{0,1:T(8,128)(2,1)S(1)}, bf16[256,2048]{0,1:T(8,128)(2,1)}, u32[]{:S(2)}) copy-start(bf16[256,2048]{0,1:T(8,128)(2,1)} %copy-done) | copy-start | bytes 3145732
  88.6 26.2 %copy-start.2 = (f32[256,8,64]{0,2,1:T(8,128)S(1)}, f32[256,8,64]{0,2,1:T(8,128)}, u32[]{:S(2)}) copy-start(f32[256,8,64]{0,2,1:T(8,128)} %convolution_bitcast_fusion) | copy-start | bytes 1572868
  88.6 26.2 %copy-start.3 = (f32[256,8,64]{0,2,1:T(8,128)S(1)}, f32[256,8,64]{0,2,1:T(8,128)}, u32[]{:S(2)}) copy-start(f32[256,8,64]{0,2,1:T(8,128)} %convolution_bitcast_fusion.1) | copy-start | bytes 1572868
  116.9 1.9 %copy-start.4 = (f32[2048]{0:T(1024)S(1)}, f32[2048]{0:T(1024)}, u32[]{:S(2)}) copy-start(f32[2048]{0:T(1024)} %param.9) | copy-start | bytes 24580
Sparse Core Ops, SparseCore 0:
  11.0 77.5 all-gather.2
where the time goes:
time: 129 us; the launch traced here: 128 us
  waiting for transfers between devices  67.2 us (52%)
  other arithmetic  30.3 us (23%)
  between operations  13.5 us (10%)
  matrix products  9.93 us (8%)
  local copies, waits for them, and re-layouts  7.12 us (6%)
    all_gather x1, waiting for transfers between devices, entering(): everything = lax.all_gather(shard.astype(jnp.bfloat16), axis)  67.2 us
    select_n x16, other arithmetic, hop(): return jnp.where(reached, new, before)  25.9 us
    unnamed x13, local copies, waits for them, and re-layouts  5.24 us
    dot_general x4, matrix products, on_device(): jnp.einsum('hts,she->the', scores, v_grp, preferred_element_type=jnp.floa...  5.01 us
    convert_element_type x1, other arithmetic, on_device(): return normed.astype(jnp.bfloat16)  2.75 us
  transfers between devices with their start and end apart: 1, of which 1 were waited for; matrix products, arithmetic and copies ran while one was open for 8% of the time, Pallas kernels for 0%

commit v1 on v0

v1 whole, which is shorter than its diff:
```python
import functools

import jax
import jax.numpy as jnp
from jax import lax
from jax.experimental import pallas as pl
from jax.experimental.pallas import tpu as pltpu
from jax.sharding import PartitionSpec as P

HEAD_DIM = 64
PAIR = 128
GRP = 256
BF = jnp.bfloat16
F32 = jnp.float32


def kernel(n, q_hbm, k_hbm, v_hbm, gain_ref, out_hbm,
           q, k, v, o, numer, st, s0, r0, cs, r1, pf, r2, s3, r3, own,
           in_sem, out_sem, c_send, c_recv, a_send, a_recv, b_send, b_recv):
    count, width = q.shape
    chips = n // 2
    half = width // 2
    per_half = half // GRP
    rows = st.shape[1] // chips
    me = lax.axis_index("seq")
    core = lax.rem(me, 2)
    chip = me // 2
    other = 1 - core
    partner = me + 1 - 2 * core

    def load(src, dst, h, sem):
        at = pl.ds(pl.multiple_of(h * half, half), half)
        return pltpu.make_async_copy(src.at[:, at], dst.at[:, at], in_sem.at[sem])

    loads = [load(k_hbm, k, other, 0), load(v_hbm, v, other, 1),
             load(k_hbm, k, core, 2), load(v_hbm, v, core, 3),
             pltpu.make_async_copy(q_hbm, q, in_sem.at[4])]
    for c in loads:
        c.start()

    barrier = pltpu.get_barrier_semaphore()
    pl.semaphore_signal(barrier, inc=1, device_id={"seq": partner},
                        device_id_type=pl.DeviceIdType.MESH)

    def greet(d, _):
        to = lax.rem(chip + d, chips) * 2 + core
        pl.semaphore_signal(barrier, inc=1, device_id={"seq": to},
                            device_id_type=pl.DeviceIdType.MESH)
        return 0

    lax.fori_loop(1, chips, greet, 0)

    lane = lax.broadcasted_iota(jnp.int32, (HEAD_DIM, PAIR), 1)
    first = lane < HEAD_DIM

    def state_group(h, g):
        at = pl.ds(pl.multiple_of(h * half + g * GRP, GRP), GRP)
        fk = jnp.maximum(k[:, at], 0)
        m = lax.dot_general(fk, v[:, at], (((0,), (0,)), ((), ())),
                            preferred_element_type=F32)
        for p in range(GRP // PAIR):
            a = p * PAIR
            blk = jnp.where(first, m[a:a + HEAD_DIM, a:a + PAIR],
                            m[a + HEAD_DIM:a + PAIR, a:a + PAIR])
            row = pl.multiple_of((g * 2 + p) * HEAD_DIM, HEAD_DIM)
            st[h, pl.ds(row, HEAD_DIM), :] = blk

    def state_half(h):
        def body(g, _):
            state_group(h, g)
            return 0
        lax.fori_loop(0, per_half, body, 0)

    loads[0].wait()
    loads[1].wait()
    state_half(other)
    s0[...] = st[other].astype(BF)

    pl.semaphore_wait(barrier, chips)

    def core_copy(src, dst, i):
        return pltpu.make_async_remote_copy(
            src_ref=src, dst_ref=dst, send_sem=c_send.at[i], recv_sem=c_recv.at[i],
            device_id={"seq": partner}, device_id_type=pl.DeviceIdType.MESH)

    x0 = core_copy(s0, r0, 0)
    x0.start()
    loads[2].wait()
    loads[3].wait()
    state_half(core)
    x0.wait_recv()
    cs[...] = (st[core] + r0[...].astype(F32)).astype(BF).reshape(cs.shape)

    def scatter(src, dst, ssem, rsem, to, slot):
        return pltpu.make_async_remote_copy(
            src_ref=src.at[to], dst_ref=dst.at[slot],
            send_sem=ssem.at[to], recv_sem=rsem.at[slot],
            device_id={"seq": to * 2 + core}, device_id_type=pl.DeviceIdType.MESH)

    def start_all(src, dst, ssem, rsem):
        def body(d, _):
            scatter(src, dst, ssem, rsem, lax.rem(chip + d, chips), chip).start()
            return 0
        lax.fori_loop(1, chips, body, 0)
        dst[chip] = src[chip]

    def recv_all(src, dst, ssem, rsem):
        def body(d, _):
            frm = lax.rem(chip + d, chips)
            scatter(src, dst, ssem, rsem, frm, frm).wait_recv()
            return 0
        lax.fori_loop(1, chips, body, 0)

    def sent_all(src, dst, ssem, rsem):
        def body(d, _):
            scatter(src, dst, ssem, rsem, lax.rem(chip + d, chips), chip).wait_send()
            return 0
        lax.fori_loop(1, chips, body, 0)

    head = lax.broadcasted_iota(jnp.int32, (count, GRP), 1) // HEAD_DIM
    causal = (lax.broadcasted_iota(jnp.int32, (count, count), 1)
              <= lax.broadcasted_iota(jnp.int32, (count, count), 0))

    def intra(g, _):
        at = pl.ds(pl.multiple_of(g * GRP, GRP), GRP)
        fq = jnp.maximum(q[:, at], 0)
        fk = jnp.maximum(k[:, at], 0)
        vv = v[:, at]
        zero = jnp.zeros_like(fq)
        acc = None
        for i in range(GRP // HEAD_DIM):
            s = lax.dot_general(jnp.where(head == i, fq, zero), fk, (((1,), (1,)), ((), ())),
                                preferred_element_type=F32)
            s = jnp.where(causal, s, 0.0).astype(BF)
            part = jnp.dot(s, jnp.where(head == i, vv, zero), preferred_element_type=F32)
            acc = part if acc is None else acc + part
        numer[:, at] = acc
        return 0

    start_all(cs, r1, a_send, a_recv)
    loads[4].wait()
    lax.fori_loop(0, per_half, intra, 0)
    recv_all(cs, r1, a_send, a_recv)

    def hop(i, acc):
        pf[i] = acc.astype(BF)
        return acc + r1[i].astype(F32)

    lax.fori_loop(0, chips, hop, jnp.zeros((rows, PAIR), F32))
    start_all(pf, r2, b_send, b_recv)
    lax.fori_loop(per_half, 2 * per_half, intra, 0)
    recv_all(pf, r2, b_send, b_recv)

    before = r2[...].reshape(own.shape).astype(F32)
    s3[...] = (before + jnp.where(core == 0, st[core], 0.0)).astype(BF)
    x3 = core_copy(s3, r3, 1)
    x3.start()
    own[...] = (before + jnp.where(core == 0, 0.0, r0[...].astype(F32))).astype(BF)

    square = (lax.broadcasted_iota(jnp.int32, (GRP, GRP), 0) // HEAD_DIM
              == lax.broadcasted_iota(jnp.int32, (GRP, GRP), 1) // HEAD_DIM)
    ones = jnp.where(square, 1.0 / HEAD_DIM, 0.0).astype(BF)

    def finish(h, prior):
        def body(g, _):
            at = pl.ds(pl.multiple_of(h * half + g * GRP, GRP), GRP)
            fq = jnp.maximum(q[:, at], 0)
            pair = [prior[pl.ds(pl.multiple_of((g * 2 + p) * HEAD_DIM, HEAD_DIM), HEAD_DIM), :]
                    for p in range(GRP // PAIR)]
            wide = jnp.concatenate(pair, axis=1)
            full = jnp.concatenate([wide] * (GRP // HEAD_DIM), axis=0)
            full = jnp.where(square, full, jnp.zeros_like(full))
            num = numer[:, at] + jnp.dot(fq, full, preferred_element_type=F32)
            mean = jnp.dot((num * num).astype(BF), ones, preferred_element_type=F32)
            o[:, at] = (num * lax.rsqrt(mean + 1e-05) * gain_ref[:, at]).astype(BF)
            return 0
        lax.fori_loop(0, per_half, body, 0)
        at = pl.ds(pl.multiple_of(h * half, half), half)
        return pltpu.make_async_copy(o.at[:, at], out_hbm.at[:, at], out_sem.at[h])

    w0 = finish(core, own)
    w0.start()
    x3.wait_recv()
    w1 = finish(other, r3)
    w1.start()
    x0.wait_send()
    x3.wait_send()
    sent_all(cs, r1, a_send, a_recv)
    sent_all(pf, r2, b_send, b_recv)
    w0.wait()
    w1.wait()


def on_device(n, queries, keys, values, gain):
    count, width = queries.shape
    chips = n // 2
    half_rows = width // 2 // PAIR * HEAD_DIM
    piece = half_rows // chips
    any_spec = pl.BlockSpec(memory_space=pl.ANY)
    vmem = pltpu.VMEM
    dma = pltpu.SemaphoreType.DMA
    return pl.pallas_call(
        functools.partial(kernel, n),
        out_shape=jax.ShapeDtypeStruct((count, width), BF),
        in_specs=[any_spec, any_spec, any_spec, pl.BlockSpec(memory_space=pltpu.VMEM)],
        out_specs=any_spec,
        scratch_shapes=[
            vmem((count, width), BF), vmem((count, width), BF), vmem((count, width), BF),
            vmem((count, width), BF), vmem((count, width), F32),
            vmem((2, half_rows, PAIR), F32),
            vmem((half_rows, PAIR), BF), vmem((half_rows, PAIR), BF),
            vmem((chips, piece, PAIR), BF), vmem((chips, piece, PAIR), BF),
            vmem((chips, piece, PAIR), BF), vmem((chips, piece, PAIR), BF),
            vmem((half_rows, PAIR), BF), vmem((half_rows, PAIR), BF), vmem((half_rows, PAIR), BF),
            dma((5,)), dma((2,)), dma((2,)), dma((2,)),
            dma((chips,)), dma((chips,)), dma((chips,)), dma((chips,)),
        ],
        compiler_params=pltpu.CompilerParams(
            collective_id=0, has_side_effects=True, vmem_limit_bytes=40 * 1024 * 1024),
    )(queries, keys, values, gain.reshape(1, width))


def solution(mesh):
    n = mesh.shape["seq"]
    rows = P(("groups", "seq"), None)
    return jax.shard_map(
        functools.partial(on_device, n), mesh=mesh,
        in_specs=(rows, rows, rows, P()), out_specs=rows, check_vma=False)
```

time: 129 us -> 26.3 us (0.20)
  waiting for transfers between devices: 67.2 us -> 0 us
  other arithmetic: 30.3 us -> 0 us
  Pallas kernels: 0 us -> 20.7 us
  between operations: 13.5 us -> 0.01 us
  matrix products: 9.93 us -> 0 us
  local copies, waits for them, and re-layouts: 7.12 us -> 5.34 us
    all_gather x1 -> x0, waiting for transfers between devices: 67.2 us -> none  [entering(): everything = lax.all_gather(shard.astype(jnp.bfloat16), axis)]
    select_n x16 -> x0, other arithmetic: 25.9 us -> none  [hop(): return jnp.where(reached, new, before)]
    pallas_call x0 -> x1, Pallas kernels: none -> 20.7 us  [on_device(): pl.pallas_call(functools.partial(kernel, n), out_shape=jax.ShapeDtypeStru...]
    dot_general x10 -> x0, matrix products: 9.93 us -> none  [the longest x4 5.01 us: on_device(): jnp.einsum('hts,she->the', scores, v_grp, preferred_element_type=jnp.floa...]
    convert_element_type x1 -> x0, other arithmetic: 2.75 us -> none  [on_device(): return normed.astype(jnp.bfloat16)]
    reshape x1 -> x0, local copies, waits for them, and re-layouts: 1.88 us -> none  [on_device(): normed = normed.reshape(count, HEADS * HEAD_DIM) * gain[None, :]]
    max x2 -> x0, other arithmetic: 1.37 us -> none  [the longest x1 1.3 us: on_device(): fq = jax.nn.relu(queries).reshape(count, HEADS, HEAD_DIM)]
    unnamed x13 -> x9, local copies, waits for them, and re-layouts: 5.24 us -> 5.34 us
  transfers between devices with their start and end apart: 1 -> 0, of which waited for: 1 -> 0; matrix products, arithmetic and copies ran while one was open for 8% -> 0% of each run, Pallas kernels for 0% -> 0%
where the time goes in v1:
time: 26.3 us; the launch traced here: 26 us
  Pallas kernels  20.7 us (79%)
  local copies, waits for them, and re-layouts  5.34 us (20%)
    pallas_call x1, Pallas kernels, on_device(): pl.pallas_call(functools.partial(kernel, n), out_shape=jax.ShapeDtypeStru...  20.7 us
    unnamed x9, local copies, waits for them, and re-layouts  5.34 us

profile of v1, /device:TPU:0, one launch (start us, length us, event | category | flops | bytes accessed | tf_op | source)
XLA Modules:
  0.0 26.0 jit_solution(16798652121722443136)
XLA Ops:
  0.0 0.0 copy-start
  0.0 1.2 %copy-done = bf16[256,2048]{1,0:T(8,128)(2,1)S(1)} copy-done((bf16[256,2048]{1,0:T(8,128)(2,1)S(1)}, bf16[256,2048]{1,0:T(8,128)(2,1)}, u32[]{:S(2)}) %copy-start) | copy-done | bytes 1048600
  1.2 0.0 copy-start.1
  1.2 1.2 %copy-done.1 = bf16[256,2048]{1,0:T(8,128)(2,1)S(1)} copy-done((bf16[256,2048]{1,0:T(8,128)(2,1)S(1)}, bf16[256,2048]{1,0:T(8,128)(2,1)}, u32[]{:S(2)}) %copy-start.1) | copy-done | bytes 1048600
  2.5 0.0 copy-start.2
  2.5 1.2 %copy-done.2 = bf16[256,2048]{1,0:T(8,128)(2,1)S(1)} copy-done((bf16[256,2048]{1,0:T(8,128)(2,1)S(1)}, bf16[256,2048]{1,0:T(8,128)(2,1)}, u32[]{:S(2)}) %copy-start.2) | copy-done | bytes 1048600
  3.7 0.0 copy-start.3
  3.7 0.7 %copy-done.3 = f32[2048]{0:T(1024)S(1)} copy-done((f32[2048]{0:T(1024)S(1)}, f32[2048]{0:T(1024)}, u32[]{:S(2)}) %copy-start.3) | copy-done | bytes 8216
  4.4 20.7 %shard_map.46 = bf16[256,2048]{1,0:T(8,128)(2,1)S(1)} custom-call(bf16[256,2048]{1,0:T(8,128)(2,1)S(1)} %copy-done, bf16[256,2048]{1,0:T(8,128)(2,1)S(1)} %copy-done.1, bf16[256,2048]{1,0:T(8,128)(2,1)S(1)} %copy-done.2, f32[1,2048]{1,0:T(1,128)S(1)} %bitcast.1), custom_call_target="tpu_custom_call" | custom-call | tf_op jit(solution)/shard_map/pallas_call | solution.py:202
  25.1 1.0 %copy.6 = bf16[256,2048]{1,0:T(8,128)(2,1)} copy(bf16[256,2048]{1,0:T(8,128)(2,1)S(1)} %shard_map.46) | data formatting | bytes 2097152
Async XLA Ops:
  0.0 1.2 %copy-start = (bf16[256,2048]{1,0:T(8,128)(2,1)S(1)}, bf16[256,2048]{1,0:T(8,128)(2,1)}, u32[]{:S(2)}) copy-start(bf16[256,2048]{1,0:T(8,128)(2,1)} %q_hbm.1) | copy-start | bytes 3145732
  1.2 1.2 %copy-start.1 = (bf16[256,2048]{1,0:T(8,128)(2,1)S(1)}, bf16[256,2048]{1,0:T(8,128)(2,1)}, u32[]{:S(2)}) copy-start(bf16[256,2048]{1,0:T(8,128)(2,1)} %k_hbm.1) | copy-start | bytes 3145732
  2.5 1.2 %copy-start.2 = (bf16[256,2048]{1,0:T(8,128)(2,1)S(1)}, bf16[256,2048]{1,0:T(8,128)(2,1)}, u32[]{:S(2)}) copy-start(bf16[256,2048]{1,0:T(8,128)(2,1)} %v_hbm.1) | copy-start | bytes 3145732
  3.7 0.7 %copy-start.3 = (f32[2048]{0:T(1024)S(1)}, f32[2048]{0:T(1024)}, u32[]{:S(2)}) copy-start(f32[2048]{0:T(1024)} %param.7) | copy-start | bytes 24580

commit v2 on v1

--- a/solution.py
+++ b/solution.py
@@ -14,9 +14,9 @@
 F32 = jnp.float32
 
 
-def kernel(n, q_hbm, k_hbm, v_hbm, gain_ref, out_hbm,
-           q, k, v, o, numer, st, s0, r0, cs, r1, pf, r2, s3, r3, own,
-           in_sem, out_sem, c_send, c_recv, a_send, a_recv, b_send, b_recv):
+def kernel(n, q_hbm, k_hbm, v_hbm, gain_ref, o,
+           q, k, v, numer, st, s0, r0, cs, r1, pf, r2, s3, r3, own,
+           in_sem, c_send, c_recv, a_send, a_recv, b_send, b_recv):
     count, width = q.shape
     chips = n // 2
     half = width // 2
@@ -175,20 +175,14 @@
             o[:, at] = (num * lax.rsqrt(mean + 1e-05) * gain_ref[:, at]).astype(BF)
             return 0
         lax.fori_loop(0, per_half, body, 0)
-        at = pl.ds(pl.multiple_of(h * half, half), half)
-        return pltpu.make_async_copy(o.at[:, at], out_hbm.at[:, at], out_sem.at[h])
-
-    w0 = finish(core, own)
-    w0.start()
+
+    finish(core, own)
     x3.wait_recv()
-    w1 = finish(other, r3)
-    w1.start()
+    finish(other, r3)
     x0.wait_send()
     x3.wait_send()
     sent_all(cs, r1, a_send, a_recv)
     sent_all(pf, r2, b_send, b_recv)
-    w0.wait()
-    w1.wait()
 
 
 def on_device(n, queries, keys, values, gain):
@@ -196,27 +190,27 @@
     chips = n // 2
     half_rows = width // 2 // PAIR * HEAD_DIM
     piece = half_rows // chips
-    any_spec = pl.BlockSpec(memory_space=pl.ANY)
+    hbm = pl.BlockSpec(memory_space=pltpu.HBM)
     vmem = pltpu.VMEM
     dma = pltpu.SemaphoreType.DMA
     return pl.pallas_call(
         functools.partial(kernel, n),
         out_shape=jax.ShapeDtypeStruct((count, width), BF),
-        in_specs=[any_spec, any_spec, any_spec, pl.BlockSpec(memory_space=pltpu.VMEM)],
-        out_specs=any_spec,
+        in_specs=[hbm, hbm, hbm, pl.BlockSpec(memory_space=pltpu.VMEM)],
+        out_specs=pl.BlockSpec(memory_space=pltpu.VMEM),
         scratch_shapes=[
             vmem((count, width), BF), vmem((count, width), BF), vmem((count, width), BF),
-            vmem((count, width), BF), vmem((count, width), F32),
+            vmem((count, width), F32),
             vmem((2, half_rows, PAIR), F32),
             vmem((half_rows, PAIR), BF), vmem((half_rows, PAIR), BF),
             vmem((chips, piece, PAIR), BF), vmem((chips, piece, PAIR), BF),
             vmem((chips, piece, PAIR), BF), vmem((chips, piece, PAIR), BF),
             vmem((half_rows, PAIR), BF), vmem((half_rows, PAIR), BF), vmem((half_rows, PAIR), BF),
-            dma((5,)), dma((2,)), dma((2,)), dma((2,)),
+            dma((5,)), dma((2,)), dma((2,)),
             dma((chips,)), dma((chips,)), dma((chips,)), dma((chips,)),
         ],
         compiler_params=pltpu.CompilerParams(
-            collective_id=0, has_side_effects=True, vmem_limit_bytes=40 * 1024 * 1024),
+            collective_id=0, has_side_effects=True, vmem_limit_bytes=62 * 1024 * 1024),
     )(queries, keys, values, gain.reshape(1, width))
 
 

time: 26.3 us -> 24.5 us (0.932)
  local copies, waits for them, and re-layouts: 5.34 us -> 2.3 us
  Pallas kernels: 20.7 us -> 22 us
    unnamed x9 -> x1, local copies, waits for them, and re-layouts: 5.34 us -> 2.3 us
    pallas_call x1, Pallas kernels: 20.7 us -> 22 us  [on_device(): pl.pallas_call(functools.partial(kernel, n), out_shape=jax.ShapeDtypeStru...]
where the time goes in v2:
time: 24.5 us; the launch traced here: 24.3 us
  Pallas kernels  22 us (90%)
  local copies, waits for them, and re-layouts  2.3 us (9%)
    pallas_call x1, Pallas kernels, on_device(): pl.pallas_call(functools.partial(kernel, n), out_shape=jax.ShapeDtypeStru...  22 us
    unnamed x1, local copies, waits for them, and re-layouts  2.3 us

profile of v2, /device:TPU:0, one launch (start us, length us, event | category | flops | bytes accessed | tf_op | source)
XLA Modules:
  0.0 24.3 jit_solution(16929102802299900730)
XLA Ops:
  0.0 22.0 %shard_map.46 = bf16[256,2048]{1,0:T(8,128)(2,1)} custom-call(bf16[256,2048]{1,0:T(8,128)(2,1)} %q_hbm.1, bf16[256,2048]{1,0:T(8,128)(2,1)} %k_hbm.1, bf16[256,2048]{1,0:T(8,128)(2,1)} %v_hbm.1, f32[1,2048]{1,0:T(1,128)} %bitcast.1), custom_call_target="tpu_custom_call" | custom-call | tf_op jit(solution)/shard_map/pallas_call | solution.py:196
  22.0 2.3 %copy.6 = bf16[256,2048]{1,0:T(8,128)(2,1)} copy(bf16[256,2048]{1,0:T(8,128)(2,1)} %shard_map.46) | data formatting | bytes 2097152

commit v3 on v2

v3 whole, which is shorter than its diff:
```python
import functools

import jax
import jax.numpy as jnp
from jax import lax
from jax.experimental import pallas as pl
from jax.experimental.pallas import tpu as pltpu
from jax.sharding import PartitionSpec as P

HEAD_DIM = 64
PAIR = 128
GRP = 256
BF = jnp.bfloat16
F32 = jnp.float32


def kernel(n, q_hbm, k_hbm, v_hbm, o,
           q, k, v, numer, st, s0, r0, cf, cy, ry, qs, r1, pf, r2, sy, qown, qother, s3, r3, own,
           in_sem, c_send, c_recv, y_send, y_recv, a_send, a_recv, b_send, b_recv):
    count, width = q.shape
    quads = n // 4
    half = width // 2
    per_half = half // GRP
    rows = qs.shape[1]
    me = lax.axis_index("seq")
    core = lax.rem(me, 2)
    side = lax.rem(me // 2, 2)
    quad = me // 4
    other = 1 - core
    across = 1 - side
    partner = me + 1 - 2 * core
    opposite = me + 2 - 4 * side

    def load(src, dst, h, sem):
        at = pl.ds(pl.multiple_of(h * half, half), half)
        return pltpu.make_async_copy(src.at[:, at], dst.at[:, at], in_sem.at[sem])

    loads = [load(k_hbm, k, other, 0), load(v_hbm, v, other, 1),
             load(k_hbm, k, core, 2), load(v_hbm, v, core, 3),
             pltpu.make_async_copy(q_hbm, q, in_sem.at[4])]
    for c in loads:
        c.start()

    barrier = pltpu.get_barrier_semaphore()
    for to in (partner, opposite):
        pl.semaphore_signal(barrier, inc=1, device_id={"seq": to},
                            device_id_type=pl.DeviceIdType.MESH)

    def greet(d, _):
        to = lax.rem(quad + d, quads) * 4 + side * 2 + core
        pl.semaphore_signal(barrier, inc=1, device_id={"seq": to},
                            device_id_type=pl.DeviceIdType.MESH)
        return 0

    lax.fori_loop(1, quads, greet, 0)

    lane = lax.broadcasted_iota(jnp.int32, (HEAD_DIM, PAIR), 1)
    first = lane < HEAD_DIM

    def state_group(h, g):
        at = pl.ds(pl.multiple_of(h * half + g * GRP, GRP), GRP)
        fk = jnp.maximum(k[:, at], 0)
        m = lax.dot_general(fk, v[:, at], (((0,), (0,)), ((), ())),
                            preferred_element_type=F32)
        for p in range(GRP // PAIR):
            a = p * PAIR
            blk = jnp.where(first, m[a:a + HEAD_DIM, a:a + PAIR],
                            m[a + HEAD_DIM:a + PAIR, a:a + PAIR])
            row = pl.multiple_of((g * 2 + p) * HEAD_DIM, HEAD_DIM)
            st[h, pl.ds(row, HEAD_DIM), :] = blk

    def state_half(h):
        def body(g, _):
            state_group(h, g)
            return 0
        lax.fori_loop(0, per_half, body, 0, unroll=True)

    loads[0].wait()
    loads[1].wait()
    state_half(other)
    s0[...] = st[other].astype(BF)

    pl.semaphore_wait(barrier, quads + 1)

    def swap(src, dst, ssem, rsem, i, to):
        return pltpu.make_async_remote_copy(
            src_ref=src, dst_ref=dst, send_sem=ssem.at[i], recv_sem=rsem.at[i],
            device_id={"seq": to}, device_id_type=pl.DeviceIdType.MESH)

    x0 = swap(s0, r0, c_send, c_recv, 0, partner)
    x0.start()
    loads[2].wait()
    loads[3].wait()
    state_half(core)
    x0.wait_recv()
    cf[...] = (st[core] + r0[...].astype(F32)).reshape(cf.shape)
    cy[...] = cf[across].astype(BF)
    y1 = swap(cy, ry, y_send, y_recv, 0, opposite)
    y1.start()

    def scatter(src, dst, ssem, rsem, to, slot):
        return pltpu.make_async_remote_copy(
            src_ref=src.at[to], dst_ref=dst.at[slot],
            send_sem=ssem.at[to], recv_sem=rsem.at[slot],
            device_id={"seq": to * 4 + side * 2 + core}, device_id_type=pl.DeviceIdType.MESH)

    def start_all(src, dst, ssem, rsem):
        def body(d, _):
            scatter(src, dst, ssem, rsem, lax.rem(quad + d, quads), quad).start()
            return 0
        lax.fori_loop(1, quads, body, 0)
        dst[quad] = src[quad]

    def recv_all(src, dst, ssem, rsem):
        def body(d, _):
            frm = lax.rem(quad + d, quads)
            scatter(src, dst, ssem, rsem, frm, frm).wait_recv()
            return 0
        lax.fori_loop(1, quads, body, 0)

    def sent_all(src, dst, ssem, rsem):
        def body(d, _):
            scatter(src, dst, ssem, rsem, lax.rem(quad + d, quads), quad).wait_send()
            return 0
        lax.fori_loop(1, quads, body, 0)

    head = lax.broadcasted_iota(jnp.int32, (count, GRP), 1) // HEAD_DIM
    causal = (lax.broadcasted_iota(jnp.int32, (count, count), 1)
              <= lax.broadcasted_iota(jnp.int32, (count, count), 0))

    def intra(g, _):
        at = pl.ds(pl.multiple_of(g * GRP, GRP), GRP)
        fq = jnp.maximum(q[:, at], 0)
        fk = jnp.maximum(k[:, at], 0)
        vv = v[:, at]
        zero = jnp.zeros_like(fq)
        acc = None
        for i in range(GRP // HEAD_DIM):
            s = lax.dot_general(jnp.where(head == i, fq, zero), fk, (((1,), (1,)), ((), ())),
                                preferred_element_type=F32)
            s = jnp.where(causal, s, 0.0).astype(BF)
            part = jnp.dot(s, jnp.where(head == i, vv, zero), preferred_element_type=F32)
            acc = part if acc is None else acc + part
        numer[:, at] = acc
        return 0

    def work(a, b):
        lax.fori_loop(a * per_half // 2, b * per_half // 2, intra, 0, unroll=True)

    loads[4].wait()
    work(0, 1)
    y1.wait_recv()
    qs[...] = (cf[side] + ry[...].astype(F32)).astype(BF).reshape(qs.shape)
    start_all(qs, r1, a_send, a_recv)
    work(1, 2)
    recv_all(qs, r1, a_send, a_recv)

    def hop(i, acc):
        pf[i] = acc.astype(BF)
        return acc + r1[i].astype(F32)

    lax.fori_loop(0, quads, hop, jnp.zeros((rows, PAIR), F32), unroll=True)
    start_all(pf, r2, b_send, b_recv)
    work(2, 3)
    recv_all(pf, r2, b_send, b_recv)
    earlier = r2[...].reshape(sy.shape).astype(F32)
    sy[...] = (earlier + jnp.where(side == 0, cf[side], 0.0)).astype(BF)
    y2 = swap(sy, qother, y_send, y_recv, 1, opposite)
    y2.start()
    qown[...] = earlier + jnp.where(side == 0, 0.0, ry[...].astype(F32))
    work(3, 4)
    y2.wait_recv()
    got = qother[...].astype(F32)
    mine = qown[...]
    before = jnp.concatenate([jnp.where(side == 0, mine, got),
                              jnp.where(side == 0, got, mine)], axis=0)

    s3[...] = (before + jnp.where(core == 0, st[core], 0.0)).astype(BF)
    x3 = swap(s3, r3, c_send, c_recv, 1, partner)
    x3.start()
    own[...] = (before + jnp.where(core == 0, 0.0, r0[...].astype(F32))).astype(BF)

    square = (lax.broadcasted_iota(jnp.int32, (GRP, GRP), 0) // HEAD_DIM
              == lax.broadcasted_iota(jnp.int32, (GRP, GRP), 1) // HEAD_DIM)
    ones = jnp.where(square, 1.0 / HEAD_DIM, 0.0).astype(BF)

    def finish(h, prior):
        def body(g, _):
            at = pl.ds(pl.multiple_of(h * half + g * GRP, GRP), GRP)
            fq = jnp.maximum(q[:, at], 0)
            pair = [prior[pl.ds(pl.multiple_of((g * 2 + p) * HEAD_DIM, HEAD_DIM), HEAD_DIM), :]
                    for p in range(GRP // PAIR)]
            wide = jnp.concatenate(pair, axis=1)
            full = jnp.concatenate([wide] * (GRP // HEAD_DIM), axis=0)
            full = jnp.where(square, full, jnp.zeros_like(full))
            num = numer[:, at] + jnp.dot(fq, full, preferred_element_type=F32)
            mean = jnp.dot((num * num).astype(BF), ones, preferred_element_type=F32)
            o[:, at] = (num * lax.rsqrt(mean + 1e-05)).astype(BF)
            return 0
        lax.fori_loop(0, per_half, body, 0, unroll=True)

    finish(core, own)
    x3.wait_recv()
    finish(other, r3)
    x0.wait_send()
    x3.wait_send()
    y1.wait_send()
    y2.wait_send()
    sent_all(qs, r1, a_send, a_recv)
    sent_all(pf, r2, b_send, b_recv)


def on_device(n, queries, keys, values, gain):
    count, width = queries.shape
    quads = n // 4
    half_rows = width // 2 // PAIR * HEAD_DIM
    quarter = half_rows // 2
    piece = quarter // quads
    hbm = pl.BlockSpec(memory_space=pltpu.HBM)
    vmem = pltpu.VMEM
    dma = pltpu.SemaphoreType.DMA
    normed = pl.pallas_call(
        functools.partial(kernel, n),
        out_shape=jax.ShapeDtypeStruct((count, width), BF),
        in_specs=[hbm] * 3,
        out_specs=pl.BlockSpec(memory_space=pltpu.VMEM),
        scratch_shapes=[
            vmem((count, width), BF), vmem((count, width), BF), vmem((count, width), BF),
            vmem((count, width), F32),
            vmem((2, half_rows, PAIR), F32),
            vmem((half_rows, PAIR), BF), vmem((half_rows, PAIR), BF),
            vmem((2, quarter, PAIR), F32), vmem((quarter, PAIR), BF), vmem((quarter, PAIR), BF),
            vmem((quads, piece, PAIR), BF), vmem((quads, piece, PAIR), BF),
            vmem((quads, piece, PAIR), BF), vmem((quads, piece, PAIR), BF),
            vmem((quarter, PAIR), BF), vmem((quarter, PAIR), F32), vmem((quarter, PAIR), BF),
            vmem((half_rows, PAIR), BF), vmem((half_rows, PAIR), BF), vmem((half_rows, PAIR), BF),
            dma((5,)), dma((2,)), dma((2,)), dma((2,)), dma((2,)),
            dma((quads,)), dma((quads,)), dma((quads,)), dma((quads,)),
        ],
        compiler_params=pltpu.CompilerParams(
            collective_id=0, has_side_effects=True, vmem_limit_bytes=52 * 1024 * 1024),
    )(queries, keys, values)
    return (normed.astype(F32) * gain[None, :]).astype(BF)


def solution(mesh):
    n = mesh.shape["seq"]
    rows = P(("groups", "seq"), None)
    return jax.shard_map(
        functools.partial(on_device, n), mesh=mesh,
        in_specs=(rows, rows, rows, P()), out_specs=rows, check_vma=False)
```

time: 24.5 us -> 23.3 us (0.951)
  local copies, waits for them, and re-layouts: 2.3 us -> 0.01 us
  other arithmetic: 0 us -> 1.19 us
  Pallas kernels: 22 us -> 21.6 us
    unnamed x1 -> x2, local copies, waits for them, and re-layouts: 2.3 us -> 0.01 us
    convert_element_type x0 -> x1, other arithmetic: none -> 1.19 us  [on_device(): return (normed.astype(F32) * gain[None, :]).astype(BF)]
    pallas_call x1, Pallas kernels: 22 us -> 21.6 us  [on_device(): pl.pallas_call(functools.partial(kernel, n), out_shape=jax.ShapeDtypeStru...]
where the time goes in v3:
time: 23.3 us; the launch traced here: 22.9 us
  Pallas kernels  21.6 us (93%)
  other arithmetic  1.19 us (5%)
    pallas_call x1, Pallas kernels, on_device(): pl.pallas_call(functools.partial(kernel, n), out_shape=jax.ShapeDtypeStru...  21.6 us
    convert_element_type x1, other arithmetic, on_device(): return (normed.astype(F32) * gain[None, :]).astype(BF)  1.19 us

profile of v3, /device:TPU:0, one launch (start us, length us, event | category | flops | bytes accessed | tf_op | source)
XLA Modules:
  0.0 22.9 jit_solution(12673882190296857583)
XLA Ops:
  0.0 0.0 copy-start
  0.0 21.6 %shard_map.46 = bf16[256,2048]{1,0:T(8,128)(2,1)S(1)} custom-call(bf16[256,2048]{1,0:T(8,128)(2,1)} %q_hbm.1, bf16[256,2048]{1,0:T(8,128)(2,1)} %k_hbm.1, bf16[256,2048]{1,0:T(8,128)(2,1)} %v_hbm.1), custom_call_target="tpu_custom_call" | custom-call | tf_op jit(solution)/shard_map/pallas_call | solution.py:222
  21.7 0.0 copy-done
  21.7 1.2 %multiply_convert_fusion = bf16[256,2048]{1,0:T(8,128)(2,1)} fusion(bf16[256,2048]{1,0:T(8,128)(2,1)S(1)} %shard_map.46, f32[2048]{0:T(1024)S(1)} %copy-done), kind=kLoop, calls=%fused_computation | loop fusion | flops 1572864 | bytes 2105344 | tf_op jit(solution)/shard_map/convert_element_type | solution.py:243
Async XLA Ops:
  0.0 21.7 %copy-start = (f32[2048]{0:T(1024)S(1)}, f32[2048]{0:T(1024)}, u32[]{:S(2)}) copy-start(f32[2048]{0:T(1024)} %param.7) | copy-start | bytes 24580

commit v4 on v2

--- a/solution.py
+++ b/solution.py
@@ -14,7 +14,7 @@
 F32 = jnp.float32
 
 
-def kernel(n, q_hbm, k_hbm, v_hbm, gain_ref, o,
+def kernel(n, q_hbm, k_hbm, v_hbm, o,
            q, k, v, numer, st, s0, r0, cs, r1, pf, r2, s3, r3, own,
            in_sem, c_send, c_recv, a_send, a_recv, b_send, b_recv):
     count, width = q.shape
@@ -69,7 +69,7 @@
         def body(g, _):
             state_group(h, g)
             return 0
-        lax.fori_loop(0, per_half, body, 0)
+        lax.fori_loop(0, per_half, body, 0, unroll=True)
 
     loads[0].wait()
     loads[1].wait()
@@ -139,7 +139,7 @@
 
     start_all(cs, r1, a_send, a_recv)
     loads[4].wait()
-    lax.fori_loop(0, per_half, intra, 0)
+    lax.fori_loop(0, per_half, intra, 0, unroll=True)
     recv_all(cs, r1, a_send, a_recv)
 
     def hop(i, acc):
@@ -148,7 +148,7 @@
 
     lax.fori_loop(0, chips, hop, jnp.zeros((rows, PAIR), F32))
     start_all(pf, r2, b_send, b_recv)
-    lax.fori_loop(per_half, 2 * per_half, intra, 0)
+    lax.fori_loop(per_half, 2 * per_half, intra, 0, unroll=True)
     recv_all(pf, r2, b_send, b_recv)
 
     before = r2[...].reshape(own.shape).astype(F32)
@@ -172,9 +172,9 @@
             full = jnp.where(square, full, jnp.zeros_like(full))
             num = numer[:, at] + jnp.dot(fq, full, preferred_element_type=F32)
             mean = jnp.dot((num * num).astype(BF), ones, preferred_element_type=F32)
-            o[:, at] = (num * lax.rsqrt(mean + 1e-05) * gain_ref[:, at]).astype(BF)
-            return 0
-        lax.fori_loop(0, per_half, body, 0)
+            o[:, at] = (num * lax.rsqrt(mean + 1e-05)).astype(BF)
+            return 0
+        lax.fori_loop(0, per_half, body, 0, unroll=True)
 
     finish(core, own)
     x3.wait_recv()
@@ -193,10 +193,10 @@
     hbm = pl.BlockSpec(memory_space=pltpu.HBM)
     vmem = pltpu.VMEM
     dma = pltpu.SemaphoreType.DMA
-    return pl.pallas_call(
+    normed = pl.pallas_call(
         functools.partial(kernel, n),
         out_shape=jax.ShapeDtypeStruct((count, width), BF),
-        in_specs=[hbm, hbm, hbm, pl.BlockSpec(memory_space=pltpu.VMEM)],
+        in_specs=[hbm] * 3,
         out_specs=pl.BlockSpec(memory_space=pltpu.VMEM),
         scratch_shapes=[
             vmem((count, width), BF), vmem((count, width), BF), vmem((count, width), BF),
@@ -210,8 +210,9 @@
             dma((chips,)), dma((chips,)), dma((chips,)), dma((chips,)),
         ],
         compiler_params=pltpu.CompilerParams(
-            collective_id=0, has_side_effects=True, vmem_limit_bytes=62 * 1024 * 1024),
-    )(queries, keys, values, gain.reshape(1, width))
+            collective_id=0, has_side_effects=True, vmem_limit_bytes=52 * 1024 * 1024),
+    )(queries, keys, values)
+    return (normed.astype(F32) * gain[None, :]).astype(BF)
 
 
 def solution(mesh):

time: 24.5 us -> 19.8 us (0.81)
  the two profiles are of different devices: /device:TPU:0 before, /device:TPU:1 now
where the time goes in v4:
time: 19.8 us; the launch traced here: 19.7 us
  Pallas kernels  18.5 us (93%)
  other arithmetic  1.19 us (6%)
    pallas_call x1, Pallas kernels, on_device(): pl.pallas_call(functools.partial(kernel, n), out_shape=jax.ShapeDtypeStru...  18.5 us
    convert_element_type x1, other arithmetic, on_device(): return (normed.astype(F32) * gain[None, :]).astype(BF)  1.19 us

profile of v4, /device:TPU:1, one launch (start us, length us, event | category | flops | bytes accessed | tf_op | source)
XLA Modules:
  0.0 19.7 jit_solution(6827865588222349083)
XLA Ops:
  0.0 0.0 copy-start
  0.0 18.5 %shard_map.46 = bf16[256,2048]{1,0:T(8,128)(2,1)S(1)} custom-call(bf16[256,2048]{1,0:T(8,128)(2,1)} %q_hbm.1, bf16[256,2048]{1,0:T(8,128)(2,1)} %k_hbm.1, bf16[256,2048]{1,0:T(8,128)(2,1)} %v_hbm.1), custom_call_target="tpu_custom_call" | custom-call | tf_op jit(solution)/shard_map/pallas_call | solution.py:196
  18.5 0.0 copy-done
  18.5 1.2 %multiply_convert_fusion = bf16[256,2048]{1,0:T(8,128)(2,1)} fusion(bf16[256,2048]{1,0:T(8,128)(2,1)S(1)} %shard_map.46, f32[2048]{0:T(1024)S(1)} %copy-done), kind=kLoop, calls=%fused_computation | loop fusion | flops 1572864 | bytes 2105344 | tf_op jit(solution)/shard_map/convert_element_type | solution.py:215
Async XLA Ops:
  0.0 18.5 %copy-start = (f32[2048]{0:T(1024)S(1)}, f32[2048]{0:T(1024)}, u32[]{:S(2)}) copy-start(f32[2048]{0:T(1024)} %param.7) | copy-start | bytes 24580
